TPU v7x, 32 devices: a whole 2x2x4 slice. The times are simulated.
32 devices in a mesh: grp: 2 (over x), feat: 16 (over z, y, core).
Axes of the slice: x: 2, y: 2, z: 4, core: 2. Of those that a mesh axis runs over, the one named last changes fastest.
Arguments:
- inputs: bfloat16 [5120, 4096], P('feat', 'grp'), parts along dimension 1, may hold values from -6 to 6
- pattern: int32 [4, 16], P(None, 'feat'), may hold values 0 or 1
- rank_mask: int32 [128], replicated, may hold values 0 or 1
- up_diag: bfloat16 [20480, 320], P('feat'), may hold values from -0.15625 to 0.15625
- up_cross: bfloat16 [4, 20480, 320], P(None, 'feat'), may hold values from -0.15625 to 0.15625
- up_left: bfloat16 [20480, 128], P('feat'), may hold values from -0.5 to 0.5
- up_right: bfloat16 [5120, 128], P('feat'), may hold values from -0.078125 to 0.078125
- down_diag: bfloat16 [5120, 1280], P('feat'), may hold values from -0.078125 to 0.078125
- down_cross: bfloat16 [4, 5120, 1280], P(None, 'feat'), may hold values from -0.078125 to 0.078125
- down_left: bfloat16 [5120, 128], P('feat'), may hold values from -0.5 to 0.5
- down_right: bfloat16 [20480, 128], P('feat'), may hold values from -0.0390625 to 0.0390625
- cotangent: bfloat16 [5120, 4096], P('feat', 'grp'), parts along dimension 1, may hold values from -6 to 6
Outputs:
- output: bfloat16 [5120, 4096], P('feat', 'grp'), parts along dimension 1
- input_grad: bfloat16 [5120, 4096], P('feat', 'grp'), parts along dimension 1
- grad_up_diag: float32 [20480, 640], P('feat', 'grp'), parts along dimension 1
- grad_up_cross: float32 [4, 20480, 640], P(None, 'feat', 'grp'), parts along dimension 2
- grad_up_left: float32 [20480, 256], P('feat', 'grp'), parts along dimension 1
- grad_up_right: float32 [5120, 256], P('feat', 'grp'), parts along dimension 1
- grad_down_diag: float32 [5120, 2560], P('feat', 'grp'), parts along dimension 1
- grad_down_cross: float32 [4, 5120, 2560], P(None, 'feat', 'grp'), parts along dimension 2
- grad_down_left: float32 [5120, 256], P('feat', 'grp'), parts along dimension 1
- grad_down_right: float32 [20480, 256], P('feat', 'grp'), parts along dimension 1
There are 2 independent parts, one for each index of `grp`. A program takes and returns all parts, laid end to end along the dimension named above; an argument that names none is the same for every part. Nothing has to cross between parts.
All inputs are finite; a program needn't handle non-finite values. No bound on the sum of `pattern` on one device may be relied on, other than what follows from the above.
Results may differ from a plain program's by a relative error of at most 0.0062.
Values may be sent and summed in bfloat16 or wider, within the bound.
A program may use at most 320 MiB of HBM per device.

v0:
```python
import jax
import jax.numpy as jnp
from jax import lax
from jax.sharding import PartitionSpec as P


def swapped(block, axis, apart):
    count = lax.axis_size(axis)
    route = []
    for low in range(count):
        high = low | 1 << apart
        if high != low and high < count:
            route += [(low, high), (high, low)]
    return lax.ppermute(block, axis, route)


def activate(values):
    return jax.nn.gelu(values, approximate=True)


def across(left, right):
    return lax.dot_general(
        left, right, (((0,), (0,)), ((), ())), preferred_element_type=jnp.float32
    )


def against(left, right):
    return lax.dot_general(
        left, right, (((1,), (1,)), ((), ())), preferred_element_type=jnp.float32
    )


def on_device(
    inputs,
    pattern,
    rank_mask,
    up_diag,
    up_cross,
    up_left,
    up_right,
    down_diag,
    down_cross,
    down_left,
    down_right,
    cotangent,
):
    levels = up_cross.shape[0]
    highest = lax.axis_size("feat").bit_length() - 1
    level_bits = [highest - levels + level for level in range(levels)]
    gate_values = pattern.astype(jnp.float32)
    gate_blocks = pattern.astype(jnp.bfloat16)[:, :, None]
    up_gated = up_cross * gate_blocks
    down_gated = down_cross * gate_blocks
    keep = rank_mask.astype(jnp.float32)[:, None]
    inputs_far = []
    up_far = []
    down_far = []
    for level in range(levels):
        received = swapped((inputs, up_gated[level], down_gated[level]), "feat", level_bits[level])
        inputs_far.append(received[0])
        up_far.append(received[1])
        down_far.append(received[2])
    pre_act = jnp.dot(up_diag, inputs, preferred_element_type=jnp.float32)
    for level in range(levels):
        pre_act = pre_act + jnp.dot(
            up_gated[level], inputs_far[level], preferred_element_type=jnp.float32
        )
    up_code = (lax.psum(across(up_right, inputs), "feat") * keep).astype(jnp.bfloat16)
    pre_act = pre_act + jnp.dot(up_left, up_code, preferred_element_type=jnp.float32)
    hidden = activate(pre_act).astype(jnp.bfloat16)
    result = jnp.dot(down_diag, hidden, preferred_element_type=jnp.float32)
    hidden_far = []
    for level in range(levels):
        neighbour = swapped(hidden, "feat", level_bits[level])
        hidden_far.append(neighbour)
        result = result + jnp.dot(down_gated[level], neighbour, preferred_element_type=jnp.float32)
    down_code = (lax.psum(across(down_right, hidden), "feat") * keep).astype(jnp.bfloat16)
    result = result + jnp.dot(down_left, down_code, preferred_element_type=jnp.float32)
    output = result.astype(jnp.bfloat16)
    down_back = (lax.psum(across(down_left, cotangent), "feat") * keep).astype(jnp.bfloat16)
    hidden_grad = across(down_diag, cotangent) + jnp.dot(
        down_right, down_back, preferred_element_type=jnp.float32
    )
    down_cross_grads = []
    for level in range(levels):
        far_cot = swapped(cotangent, "feat", level_bits[level])
        hidden_grad = hidden_grad + across(down_far[level], far_cot)
        down_cross_grads.append(gate_values[level, 0] * against(cotangent, hidden_far[level]))
    pre_grad = jax.vjp(activate, pre_act)[1](hidden_grad)[0].astype(jnp.bfloat16)
    up_back = (lax.psum(across(up_left, pre_grad), "feat") * keep).astype(jnp.bfloat16)
    in_grad = across(up_diag, pre_grad) + jnp.dot(
        up_right, up_back, preferred_element_type=jnp.float32
    )
    for level in range(levels):
        far_grad = swapped(pre_grad, "feat", level_bits[level])
        in_grad = in_grad + across(up_far[level], far_grad)
    input_grad = in_grad.astype(jnp.bfloat16)
    grad_up_diag = against(pre_grad, inputs)
    grad_up_cross = jnp.stack(
        [gate_values[level, 0] * against(pre_grad, inputs_far[level]) for level in range(levels)]
    )
    grad_up_left = against(pre_grad, up_code)
    grad_up_right = against(inputs, up_back)
    grad_down_diag = against(cotangent, hidden)
    grad_down_cross = jnp.stack(down_cross_grads)
    grad_down_left = against(cotangent, down_code)
    grad_down_right = against(hidden, down_back)
    return (
        output,
        input_grad,
        grad_up_diag,
        grad_up_cross,
        grad_up_left,
        grad_up_right,
        grad_down_diag,
        grad_down_cross,
        grad_down_left,
        grad_down_right,
    )


def solution(mesh):
    in_specs = (
        P("feat", "grp"),
        P(None, "feat"),
        P(),
        P("feat", None),
        P(None, "feat", None),
        P("feat", None),
        P("feat", None),
        P("feat", None),
        P(None, "feat", None),
        P("feat", None),
        P("feat", None),
        P("feat", "grp"),
    )
    out_specs = (
        P("feat", "grp"),
        P("feat", "grp"),
        P("feat", "grp"),
        P(None, "feat", "grp"),
        P("feat", "grp"),
        P("feat", "grp"),
        P("feat", "grp"),
        P(None, "feat", "grp"),
        P("feat", "grp"),
        P("feat", "grp"),
    )
    return jax.shard_map(
        on_device, mesh=mesh, in_specs=in_specs, out_specs=out_specs, check_vma=False
    )
```

profile of v0, /device:TPU:0, one launch (start us, length us, event | category | flops | bytes accessed | tf_op | source)
XLA Modules:
  0.0 959.8 jit_solution(9010921354594521081)
XLA Ops:
  28.0 5.5 fusion.42
  33.5 5.7 fusion.44
  39.9 84.3 %all-reduce.7.cloned.1.call-done = (f32[128,2048]{1,0:T(8,128)}, f32[128,2048]{1,0:T(8,128)}) async-done(((f32[128,2048]{1,0:T(8,128)}, f32[128,2048]{1,0:T(8,128)}), (f32[128,2048]{1,0:T(8,128)}, f32[128,2048]{1,0:T(8,128)})) %all-reduce.7.cloned.1.call-update) | async-done | bytes 2097168 | tf_op jit(solution)/shard_map/psum | solution.py:68
  124.2 6.9 fusion.30
  131.1 5.5 fusion.32
  138.2 6.8 fusion.33
  145.1 6.9 fusion.34
  153.0 6.8 fusion.35
  162.5 6.8 fusion.46
  175.6 7.2 fusion.47
  182.8 30.3 %collective-permute-done.12 = bf16[320,1280]{1,0:T(8,128)(2,1)S(1)} collective-permute-done((bf16[320,1280]{1,0:T(8,128)(2,1)S(1)}, bf16[320,1280]{1,0:T(8,128)(2,1)S(1)}, u32[]{:S(2)}, u32[]{:S(2)}) %collective-permute-start.12) | collective-permute-done | bytes 819232 | tf_op jit(solution)/shard_map/ppermute | solution.py:14
  213.1 5.5 fusion.48
  218.6 92.4 %collective-permute-done.14 = bf16[320,1280]{1,0:T(8,128)(2,1)S(1)} collective-permute-done((bf16[320,1280]{1,0:T(8,128)(2,1)S(1)}, bf16[320,1280]{1,0:T(8,128)(2,1)S(1)}, u32[]{:S(2)}, u32[]{:S(2)}) %collective-permute-start.14) | collective-permute-done | bytes 819232 | tf_op jit(solution)/shard_map/ppermute | solution.py:14
  311.0 5.7 fusion.49
  316.7 41.7 %fusion.6 = (bf16[1280,2048]{1,0:T(8,128)(2,1)}, bf16[1280,2048]{1,0:T(8,128)(2,1)}) fusion(f32[1280,2048]{1,0:T(8,128)} %fusion.49, f32[1280,2048]{1,0:T(8,128)} %fusion.48, f32[1280,2048]{1,0:T(8,128)} %fusion.47, f32[1280,2048]{1,0:T(8,128)} %fusion.46, f32[1280,2048]{1,0:T(8,128)} %fusion.44, f32[2048,1280]{0,1:T(8,128)} %fusion.32, ...), kind=kOutput, calls=%fused_computation.8 | convolution fusion | flops 1761607680 | bytes 127959040 | tf_op jit(solution)/shard_map/dot_general | solution.py:65
  370.9 5.9 fusion.54
  377.8 5.7 fusion.12
  383.6 5.5 fusion.11
  392.5 5.5 fusion.13
  398.0 5.3 fusion.14
  406.6 5.6 fusion.53
  412.2 4.9 fusion.29
  422.7 245.8 %all-reduce.5.cloned.1.call-done = (f32[128,2048]{1,0:T(8,128)}, f32[128,2048]{1,0:T(8,128)}) async-done(((f32[128,2048]{1,0:T(8,128)}, f32[128,2048]{1,0:T(8,128)}), (f32[128,2048]{1,0:T(8,128)}, f32[128,2048]{1,0:T(8,128)})) %all-reduce.5.cloned.1.call-update) | async-done | bytes 2097168 | tf_op jit(solution)/shard_map/psum | solution.py:77
  682.3 5.0 fusion.16
  687.3 5.3 fusion.17
  692.7 4.4 fusion.38
  697.1 5.0 fusion.18
  703.1 5.9 fusion.39
  709.0 5.1 fusion.15
  714.1 8.7 collective-permute-done.18
  732.5 201.0 %collective-permute-done.20 = bf16[1280,320]{0,1:T(8,128)(2,1)S(1)} collective-permute-done((bf16[1280,320]{0,1:T(8,128)(2,1)S(1)}, bf16[1280,320]{0,1:T(8,128)(2,1)S(1)}, u32[]{:S(2)}, u32[]{:S(2)}) %collective-permute-start.20) | collective-permute-done | bytes 819232 | tf_op jit(solution)/shard_map/ppermute | solution.py:14
  942.5 6.8 fusion.27
  (140 shorter events, 95.3 us)
Async XLA Ops:
  7.2 20.8 %copy-start = (bf16[1280,320]{0,1:T(8,128)(2,1)S(1)}, bf16[1280,320]{0,1:T(8,128)(2,1)}, u32[]{:S(2)}) copy-start(bf16[1280,320]{0,1:T(8,128)(2,1)} %param.15) | copy-start | bytes 2457604
  7.2 116.9 %all-reduce.7.cloned.1.call-start = ((), (), s32[]{:S(2)}) async-start(), calls=%async_computation.1 | async-start | bytes 4194304 | tf_op jit(solution)/shard_map/psum | solution.py:68
  7.3 154.0 %collective-permute-start.9 = (bf16[320,2048]{1,0:T(8,128)(2,1)}, bf16[320,2048]{1,0:T(8,128)(2,1)}, u32[]{:S(2)}, u32[]{:S(2)}) collective-permute-start(bf16[320,2048]{1,0:T(8,128)(2,1)} %param.23), channel_id=1, source_target_pairs={{0,1},{1,0},{2,3},{3,2},{4,5},{5,4},{6,7},{7,6},{8,9},{9,8},{10,11... | collective-permute-start | bytes 3932168 | tf_op jit(solution)/shard_map/ppermute | solution.py:14
  7.8 166.4 %collective-permute-start.11 = (bf16[320,2048]{1,0:T(8,128)(2,1)}, bf16[320,2048]{1,0:T(8,128)(2,1)}, u32[]{:S(2)}, u32[]{:S(2)}) collective-permute-start(bf16[320,2048]{1,0:T(8,128)(2,1)} %param.23), channel_id=1, source_target_pairs={{0,2},{2,0},{1,3},{3,1},{4,6},{6,4},{5,7},{7,5},{8,10},{10,8},{9,1... | collective-permute-start | bytes 3932168 | tf_op jit(solution)/shard_map/ppermute | solution.py:14
  10.4 126.2 %collective-permute-start = (bf16[320,2048]{1,0:T(8,128)(2,1)}, bf16[320,2048]{1,0:T(8,128)(2,1)}, u32[]{:S(2)}, u32[]{:S(2)}) collective-permute-start(bf16[320,2048]{1,0:T(8,128)(2,1)} %param.12), channel_id=1, source_target_pairs={{0,1},{1,0},{2,3},{3,2},{4,5},{5,4},{6,7},{7,6},{8,9},{9,8},{10,11... | collective-permute-start | bytes 3932168 | tf_op jit(solution)/shard_map/ppermute | solution.py:14
  10.5 134.5 %collective-permute-start.1 = (bf16[320,2048]{1,0:T(8,128)(2,1)}, bf16[320,2048]{1,0:T(8,128)(2,1)}, u32[]{:S(2)}, u32[]{:S(2)}) collective-permute-start(bf16[320,2048]{1,0:T(8,128)(2,1)} %param.12), channel_id=1, source_target_pairs={{0,2},{2,0},{1,3},{3,1},{4,6},{6,4},{5,7},{7,5},{8,10},{10,8},{9,1... | collective-permute-start | bytes 3932168 | tf_op jit(solution)/shard_map/ppermute | solution.py:14
  10.8 141.2 %collective-permute-start.2 = (bf16[320,2048]{1,0:T(8,128)(2,1)}, bf16[320,2048]{1,0:T(8,128)(2,1)}, u32[]{:S(2)}, u32[]{:S(2)}) collective-permute-start(bf16[320,2048]{1,0:T(8,128)(2,1)} %param.12), channel_id=1, source_target_pairs={{0,4},{4,0},{1,5},{5,1},{2,6},{6,2},{3,7},{7,3},{8,12},{12,8},{9,1... | collective-permute-start | bytes 3932168 | tf_op jit(solution)/shard_map/ppermute | solution.py:14
  17.8 650.6 %all-reduce.5.cloned.1.call-start = ((), (), s32[]{:S(2)}) async-start(), calls=%async_computation | async-start | bytes 4194304 | tf_op jit(solution)/shard_map/psum | solution.py:77
  136.6 76.5 %collective-permute-start.13 = (bf16[320,2048]{1,0:T(8,128)(2,1)S(1)}, bf16[320,2048]{1,0:T(8,128)(2,1)S(1)}, u32[]{:S(2)}, u32[]{:S(2)}) collective-permute-start(bf16[320,2048]{1,0:T(8,128)(2,1)S(1)} %copy-done.7), channel_id=1, source_target_pairs={{0,4},{4,0},{1,5},{5,1},{2,6},{6,2},{3,7},{7,3},{8,12},{12,8},{9,1... | collective-permute-start | bytes 3932168 | tf_op jit(solution)/shard_map/ppermute | solution.py:14
  145.0 14.8 %collective-permute-start.8 = (bf16[320,1280]{1,0:T(8,128)(2,1)S(1)}, bf16[320,1280]{1,0:T(8,128)(2,1)S(1)}, u32[]{:S(2)}, u32[]{:S(2)}) collective-permute-start(bf16[320,1280]{1,0:T(8,128)(2,1)S(1)} %copy-done.26), channel_id=1, source_target_pairs={{0,1},{1,0},{2,3},{3,2},{4,5},{5,4},{6,7},{7,6},{8,9},{9,8},{10,11... | collective-permute-start | bytes 2457608 | tf_op jit(solution)/shard_map/ppermute | solution.py:14
  152.0 20.7 %collective-permute-start.10 = (bf16[320,1280]{1,0:T(8,128)(2,1)S(1)}, bf16[320,1280]{1,0:T(8,128)(2,1)S(1)}, u32[]{:S(2)}, u32[]{:S(2)}) collective-permute-start(bf16[320,1280]{1,0:T(8,128)(2,1)S(1)} %copy-done.25), channel_id=1, source_target_pairs={{0,2},{2,0},{1,3},{3,1},{4,6},{6,4},{5,7},{7,5},{8,10},{10,8},{9,1... | collective-permute-start | bytes 2457608 | tf_op jit(solution)/shard_map/ppermute | solution.py:14
  159.8 151.2 %collective-permute-start.15 = (bf16[320,2048]{1,0:T(8,128)(2,1)S(1)}, bf16[320,2048]{1,0:T(8,128)(2,1)S(1)}, u32[]{:S(2)}, u32[]{:S(2)}) collective-permute-start(bf16[320,2048]{1,0:T(8,128)(2,1)S(1)} %copy-done.7), channel_id=1, source_target_pairs={{0,8},{8,0},{1,9},{9,1},{2,10},{10,2},{3,11},{11,3},{4,12},{12,4},... | collective-permute-start | bytes 3932168 | tf_op jit(solution)/shard_map/ppermute | solution.py:14
  161.3 51.8 %collective-permute-start.12 = (bf16[320,1280]{1,0:T(8,128)(2,1)S(1)}, bf16[320,1280]{1,0:T(8,128)(2,1)S(1)}, u32[]{:S(2)}, u32[]{:S(2)}) collective-permute-start(bf16[320,1280]{1,0:T(8,128)(2,1)S(1)} %copy-done.24), channel_id=1, source_target_pairs={{0,4},{4,0},{1,5},{5,1},{2,6},{6,2},{3,7},{7,3},{8,12},{12,8},{9,1... | collective-permute-start | bytes 2457608 | tf_op jit(solution)/shard_map/ppermute | solution.py:14
  172.7 144.0 %collective-permute-start.3 = (bf16[320,2048]{1,0:T(8,128)(2,1)S(1)}, bf16[320,2048]{1,0:T(8,128)(2,1)}, u32[]{:S(2)}, u32[]{:S(2)}) collective-permute-start(bf16[320,2048]{1,0:T(8,128)(2,1)S(1)} %copy-done.6), channel_id=1, source_target_pairs={{0,8},{8,0},{1,9},{9,1},{2,10},{10,2},{3,11},{11,3},{4,12},{12,4},... | collective-permute-start | bytes 3932168 | tf_op jit(solution)/shard_map/ppermute | solution.py:14
  174.1 136.9 %collective-permute-start.14 = (bf16[320,1280]{1,0:T(8,128)(2,1)S(1)}, bf16[320,1280]{1,0:T(8,128)(2,1)S(1)}, u32[]{:S(2)}, u32[]{:S(2)}) collective-permute-start(bf16[320,1280]{1,0:T(8,128)(2,1)S(1)} %copy-done.23), channel_id=1, source_target_pairs={{0,8},{8,0},{1,9},{9,1},{2,10},{10,2},{3,11},{11,3},{4,12},{12,4},... | collective-permute-start | bytes 2457608 | tf_op jit(solution)/shard_map/ppermute | solution.py:14
  358.4 343.7 %collective-permute-start.4 = (bf16[1280,2048]{1,0:T(8,128)(2,1)}, bf16[1280,2048]{1,0:T(8,128)(2,1)}, u32[]{:S(2)}, u32[]{:S(2)}) collective-permute-start(bf16[1280,2048]{1,0:T(8,128)(2,1)} %get-tuple-element.15), channel_id=1, source_target_pairs={{0,1},{1,0},{2,3},{3,2},{4,5},{5,4},{6,7},{7,6},{8,9},{9,8},{10,11... | collective-permute-start | bytes 15728648 | tf_op jit(solution)/shard_map/ppermute | solution.py:14
  358.5 315.0 %collective-permute-start.5 = (bf16[1280,2048]{1,0:T(8,128)(2,1)}, bf16[1280,2048]{1,0:T(8,128)(2,1)}, u32[]{:S(2)}, u32[]{:S(2)}) collective-permute-start(bf16[1280,2048]{1,0:T(8,128)(2,1)} %get-tuple-element.15), channel_id=1, source_target_pairs={{0,2},{2,0},{1,3},{3,1},{4,6},{6,4},{5,7},{7,5},{8,10},{10,8},{9,1... | collective-permute-start | bytes 15728648 | tf_op jit(solution)/shard_map/ppermute | solution.py:14
  359.7 316.8 %collective-permute-start.6 = (bf16[1280,2048]{1,0:T(8,128)(2,1)}, bf16[1280,2048]{1,0:T(8,128)(2,1)}, u32[]{:S(2)}, u32[]{:S(2)}) collective-permute-start(bf16[1280,2048]{1,0:T(8,128)(2,1)} %get-tuple-element.15), channel_id=1, source_target_pairs={{0,4},{4,0},{1,5},{5,1},{2,6},{6,2},{3,7},{7,3},{8,12},{12,8},{9,1... | collective-permute-start | bytes 15728648 | tf_op jit(solution)/shard_map/ppermute | solution.py:14
  359.7 332.9 %collective-permute-start.7 = (bf16[1280,2048]{1,0:T(8,128)(2,1)}, bf16[1280,2048]{1,0:T(8,128)(2,1)}, u32[]{:S(2)}, u32[]{:S(2)}) collective-permute-start(bf16[1280,2048]{1,0:T(8,128)(2,1)} %get-tuple-element.15), channel_id=1, source_target_pairs={{0,8},{8,0},{1,9},{9,1},{2,10},{10,2},{3,11},{11,3},{4,12},{12,4},... | collective-permute-start | bytes 15728648 | tf_op jit(solution)/shard_map/ppermute | solution.py:14
  376.8 347.1 %collective-permute-start.19 = (bf16[1280,2048]{1,0:T(8,128)(2,1)}, bf16[1280,2048]{1,0:T(8,128)(2,1)}, u32[]{:S(2)}, u32[]{:S(2)}) collective-permute-start(bf16[1280,2048]{1,0:T(8,128)(2,1)} %get-tuple-element.14), channel_id=1, source_target_pairs={{0,2},{2,0},{1,3},{3,1},{4,6},{6,4},{5,7},{7,5},{8,10},{10,8},{9,1... | collective-permute-start | bytes 15728648 | tf_op jit(solution)/shard_map/ppermute | solution.py:14
  420.2 250.9 %copy-start.27 = (bf16[320,128]{1,0:T(8,128)(2,1)S(1)}, bf16[320,128]{1,0:T(8,128)(2,1)}, u32[]{:S(2)}) copy-start(bf16[320,128]{1,0:T(8,128)(2,1)} %param.21) | copy-start | bytes 245764
  422.7 250.2 %copy-start.28 = (bf16[320,128]{1,0:T(8,128)(2,1)S(1)}, bf16[320,128]{1,0:T(8,128)(2,1)}, u32[]{:S(2)}) copy-start(bf16[320,128]{1,0:T(8,128)(2,1)} %param.18) | copy-start | bytes 245764
  673.5 260.0 %collective-permute-start.21 = (bf16[1280,2048]{1,0:T(8,128)(2,1)}, bf16[1280,2048]{1,0:T(8,128)(2,1)S(1)}, u32[]{:S(2)}, u32[]{:S(2)}) collective-permute-start(bf16[1280,2048]{1,0:T(8,128)(2,1)} %get-tuple-element.14), channel_id=1, source_target_pairs={{0,4},{4,0},{1,5},{5,1},{2,6},{6,2},{3,7},{7,3},{8,12},{12,8},{9,1... | collective-permute-start | bytes 15728648 | tf_op jit(solution)/shard_map/ppermute | solution.py:14
  676.4 261.7 %collective-permute-start.23 = (bf16[1280,2048]{1,0:T(8,128)(2,1)}, bf16[1280,2048]{1,0:T(8,128)(2,1)}, u32[]{:S(2)}, u32[]{:S(2)}) collective-permute-start(bf16[1280,2048]{1,0:T(8,128)(2,1)} %get-tuple-element.14), channel_id=1, source_target_pairs={{0,8},{8,0},{1,9},{9,1},{2,10},{10,2},{3,11},{11,3},{4,12},{12,4},... | collective-permute-start | bytes 15728648 | tf_op jit(solution)/shard_map/ppermute | solution.py:14
  692.6 256.8 %collective-permute-start.17 = (bf16[1280,2048]{1,0:T(8,128)(2,1)}, bf16[1280,2048]{1,0:T(8,128)(2,1)S(1)}, u32[]{:S(2)}, u32[]{:S(2)}) collective-permute-start(bf16[1280,2048]{1,0:T(8,128)(2,1)} %get-tuple-element.14), channel_id=1, source_target_pairs={{0,1},{1,0},{2,3},{3,2},{4,5},{5,4},{6,7},{7,6},{8,9},{9,8},{10,11... | collective-permute-start | bytes 15728648 | tf_op jit(solution)/shard_map/ppermute | solution.py:14
  702.1 20.7 %collective-permute-start.18 = (bf16[1280,320]{0,1:T(8,128)(2,1)S(1)}, bf16[1280,320]{0,1:T(8,128)(2,1)S(1)}, u32[]{:S(2)}, u32[]{:S(2)}) collective-permute-start(bf16[1280,320]{0,1:T(8,128)(2,1)S(1)} %copy-done.22), channel_id=1, source_target_pairs={{0,2},{2,0},{1,3},{3,1},{4,6},{6,4},{5,7},{7,5},{8,10},{10,8},{9,1... | collective-permute-start | bytes 2457608 | tf_op jit(solution)/shard_map/ppermute | solution.py:14
  709.0 13.8 %copy-start.21 = (bf16[1280,320]{0,1:T(8,128)(2,1)S(1)}, bf16[1280,320]{0,1:T(8,128)(2,1)}, u32[]{:S(2)}) copy-start(bf16[1280,320]{0,1:T(8,128)(2,1)} %get-tuple-element.18) | copy-start | bytes 2457604
  709.0 14.9 %copy-start.20 = (bf16[1280,320]{0,1:T(8,128)(2,1)S(1)}, bf16[1280,320]{0,1:T(8,128)(2,1)}, u32[]{:S(2)}) copy-start(bf16[1280,320]{0,1:T(8,128)(2,1)} %get-tuple-element.17) | copy-start | bytes 2457604
  722.8 210.7 %collective-permute-start.20 = (bf16[1280,320]{0,1:T(8,128)(2,1)S(1)}, bf16[1280,320]{0,1:T(8,128)(2,1)S(1)}, u32[]{:S(2)}, u32[]{:S(2)}) collective-permute-start(bf16[1280,320]{0,1:T(8,128)(2,1)S(1)} %copy-done.21), channel_id=1, source_target_pairs={{0,4},{4,0},{1,5},{5,1},{2,6},{6,2},{3,7},{7,3},{8,12},{12,8},{9,1... | collective-permute-start | bytes 2457608 | tf_op jit(solution)/shard_map/ppermute | solution.py:14
  723.9 214.3 %collective-permute-start.22 = (bf16[1280,320]{0,1:T(8,128)(2,1)S(1)}, bf16[1280,320]{0,1:T(8,128)(2,1)S(1)}, u32[]{:S(2)}, u32[]{:S(2)}) collective-permute-start(bf16[1280,320]{0,1:T(8,128)(2,1)S(1)} %copy-done.20), channel_id=1, source_target_pairs={{0,8},{8,0},{1,9},{9,1},{2,10},{10,2},{3,11},{11,3},{4,12},{12,4},... | collective-permute-start | bytes 2457608 | tf_op jit(solution)/shard_map/ppermute | solution.py:14
  729.2 204.3 %copy-start.19 = (bf16[1280,320]{0,1:T(8,128)(2,1)S(1)}, bf16[1280,320]{0,1:T(8,128)(2,1)}, u32[]{:S(2)}) copy-start(bf16[1280,320]{0,1:T(8,128)(2,1)} %get-tuple-element.16) | copy-start | bytes 2457604
  933.5 15.9 %collective-permute-start.16 = (bf16[1280,320]{0,1:T(8,128)(2,1)S(1)}, bf16[1280,320]{0,1:T(8,128)(2,1)S(1)}, u32[]{:S(2)}, u32[]{:S(2)}) collective-permute-start(bf16[1280,320]{0,1:T(8,128)(2,1)S(1)} %copy-done.19), channel_id=1, source_target_pairs={{0,1},{1,0},{2,3},{3,2},{4,5},{5,4},{6,7},{7,6},{8,9},{9,8},{10,11... | collective-permute-start | bytes 2457608 | tf_op jit(solution)/shard_map/ppermute | solution.py:14
  (27 other events, 167.5 us)
Sparse Core Ops, SparseCore 0:
  17.9 106.1 all-reduce.6
  377.9 290.4 all-reduce.4
where the time goes:
time: 970 us; the launch traced here: 960 us
  waiting for transfers between devices  669 us (69%)
  matrix products  234 us (24%)
  starting transfers between devices  24.4 us (3%)
  between operations  15 us (2%)
    ppermute x24, waiting for transfers between devices, swapped(): return lax.ppermute(block, axis, route)  339 us
    psum x1, waiting for transfers between devices, on_device(): lax.psum(across(down_right, hidden), 'feat') * keep  246 us
    psum x1, waiting for transfers between devices, on_device(): lax.psum(across(up_right, inputs), 'feat') * keep  84.3 us
    dot_general x14, matrix products, across(): lax.dot_general(left, right, (((0,), (0,)), ((), ())), preferred_element_...  64.4 us
    dot_general x14, matrix products, against(): lax.dot_general(left, right, (((1,), (1,)), ((), ())), preferred_element_...  62.4 us
    dot_general x4, matrix products, on_device(): jnp.dot(up_gated[level], inputs_far[level], preferred_element_type=jnp.fl...  62.3 us
    ppermute x24, starting transfers between devices, swapped(): return lax.ppermute(block, axis, route)  24.3 us
    dot_general x4, matrix products, on_device(): jnp.dot(down_gated[level], neighbour, preferred_element_type=jnp.float32)  21.6 us
  transfers between devices with their start and end apart: 26, of which 8 were waited for; matrix products, arithmetic and copies ran while one was open for 21% of the time, Pallas kernels for 0%

commit v1 on v0

--- a/solution.py
+++ b/solution.py
@@ -65,7 +65,9 @@
         pre_act = pre_act + jnp.dot(
             up_gated[level], inputs_far[level], preferred_element_type=jnp.float32
         )
-    up_code = (lax.psum(across(up_right, inputs), "feat") * keep).astype(jnp.bfloat16)
+    up_code = (jnp.sum(lax.all_gather(across(up_right, inputs), "feat"), axis=0) * keep).astype(
+        jnp.bfloat16
+    )
     pre_act = pre_act + jnp.dot(up_left, up_code, preferred_element_type=jnp.float32)
     hidden = activate(pre_act).astype(jnp.bfloat16)
     result = jnp.dot(down_diag, hidden, preferred_element_type=jnp.float32)

time: 970 us -> 1050 us (1.082)
  waiting for transfers between devices: 669 us -> 743 us
    ppermute x24, waiting for transfers between devices: 339 us -> 426 us  [swapped(): return lax.ppermute(block, axis, route)]
    psum x1, waiting for transfers between devices: 84.3 us -> 71.2 us  [on_device(): lax.psum(across(down_left, cotangent), 'feat') * keep]
  transfers between devices with their start and end apart: 26 -> 27, of which waited for: 8 -> 8; matrix products, arithmetic and copies ran while one was open for 21% -> 20% of each run, Pallas kernels for 0% -> 0%
where the time goes in v1:
time: 1050 us
  waiting for transfers between devices  743 us (71%)
  matrix products  237 us (23%)
  starting transfers between devices  23.3 us (2%)
  other arithmetic  17.3 us (2%)
  between operations  14.5 us (1%)
  local copies, waits for them, and re-layouts  10.9 us (1%)
    ppermute x24, waiting for transfers between devices, swapped(): return lax.ppermute(block, axis, route)  426 us
    psum x1, waiting for transfers between devices, on_device(): lax.psum(across(down_right, hidden), 'feat') * keep  246 us
    psum x1, waiting for transfers between devices, on_device(): lax.psum(across(down_left, cotangent), 'feat') * keep  71.2 us
    dot_general x14, matrix products, across(): lax.dot_general(left, right, (((0,), (0,)), ((), ())), preferred_element_...  65.1 us
    dot_general x4, matrix products, on_device(): jnp.dot(up_gated[level], inputs_far[level], preferred_element_type=jnp.fl...  62.8 us
    dot_general x14, matrix products, against(): lax.dot_general(left, right, (((1,), (1,)), ((), ())), preferred_element_...  62.4 us
    ppermute x24, starting transfers between devices, swapped(): return lax.ppermute(block, axis, route)  23.2 us
    dot_general x4, matrix products, on_device(): jnp.dot(down_gated[level], neighbour, preferred_element_type=jnp.float32)  21.6 us
  transfers between devices with their start and end apart: 27, of which 8 were waited for; matrix products, arithmetic and copies ran while one was open for 20% of the time, Pallas kernels for 0%

profile of v1, /device:TPU:0, one launch (start us, length us, event | category | flops | bytes accessed | tf_op | source)
XLA Modules:
  0.0 1046.7 jit_solution(18029016887362802727)
XLA Ops:
  27.7 5.8 fusion.42
  33.5 5.7 fusion.44
  39.9 71.2 %all-reduce.4.cloned.1.call-done = f32[128,2048]{0,1:T(8,128)} async-done(((f32[128,2048]{0,1:T(8,128)}), f32[128,2048]{0,1:T(8,128)}) %all-reduce.4.cloned.1.call-update) | async-done | bytes 1048592 | tf_op jit(solution)/shard_map/psum | solution.py:82
  111.1 6.9 fusion.32
  119.7 6.9 fusion.33
  126.7 6.8 fusion.34
  134.1 6.8 fusion.35
  144.0 6.9 fusion.46
  157.2 6.9 fusion.47
  164.0 101.6 %collective-permute-done.12 = bf16[320,1280]{1,0:T(8,128)(2,1)S(1)} collective-permute-done((bf16[320,1280]{1,0:T(8,128)(2,1)S(1)}, bf16[320,1280]{1,0:T(8,128)(2,1)S(1)}, u32[]{:S(2)}, u32[]{:S(2)}) %collective-permute-start.12) | collective-permute-done | bytes 819232 | tf_op jit(solution)/shard_map/ppermute | solution.py:14
  265.7 5.8 fusion.48
  271.5 108.6 %collective-permute-done.14 = bf16[320,1280]{1,0:T(8,128)(2,1)S(1)} collective-permute-done((bf16[320,1280]{1,0:T(8,128)(2,1)S(1)}, bf16[320,1280]{1,0:T(8,128)(2,1)S(1)}, u32[]{:S(2)}, u32[]{:S(2)}) %collective-permute-start.14) | collective-permute-done | bytes 819232 | tf_op jit(solution)/shard_map/ppermute | solution.py:14
  380.0 5.5 fusion.49
  385.6 8.4 reduce_sum.9
  396.5 6.9 fusion.30
  403.4 42.3 %fusion.6 = (bf16[1280,2048]{1,0:T(8,128)(2,1)}, bf16[1280,2048]{1,0:T(8,128)(2,1)}) fusion(f32[1280,2048]{1,0:T(8,128)} %fusion.49, f32[1280,2048]{1,0:T(8,128)} %fusion.48, f32[1280,2048]{1,0:T(8,128)} %fusion.47, f32[1280,2048]{1,0:T(8,128)} %fusion.46, f32[1280,2048]{1,0:T(8,128)} %fusion.44, f32[2048,1280]{0,1:T(8,128)} %fusion.32, ...), kind=kOutput, calls=%fused_computation.8 | convolution fusion | flops 1761607680 | bytes 127959040 | tf_op jit(solution)/shard_map/dot_general | solution.py:65
  448.8 5.1 convolution_bitcast_fusion.4
  453.8 5.0 convolution_bitcast_fusion.3
  458.9 5.8 fusion.54
  465.0 5.7 fusion.12
  470.7 5.6 fusion.11
  479.7 5.3 fusion.13
  485.1 5.6 fusion.14
  493.8 5.6 fusion.53
  509.8 246.2 %all-reduce.6.cloned.1.call-done = (f32[128,2048]{0,1:T(8,128)}, f32[128,2048]{0,1:T(8,128)}) async-done(((f32[128,2048]{0,1:T(8,128)}, f32[128,2048]{0,1:T(8,128)}), (f32[128,2048]{0,1:T(8,128)}, f32[128,2048]{0,1:T(8,128)})) %all-reduce.6.cloned.1.call-update) | async-done | bytes 2097168 | tf_op jit(solution)/shard_map/psum | solution.py:79
  774.6 5.2 fusion.17
  784.3 5.1 fusion.18
  790.4 5.9 fusion.39
  796.4 5.1 fusion.15
  801.5 8.7 collective-permute-done.18
  819.9 201.1 %collective-permute-done.20 = bf16[1280,320]{0,1:T(8,128)(2,1)S(1)} collective-permute-done((bf16[1280,320]{0,1:T(8,128)(2,1)S(1)}, bf16[1280,320]{0,1:T(8,128)(2,1)S(1)}, u32[]{:S(2)}, u32[]{:S(2)}) %collective-permute-start.20) | collective-permute-done | bytes 819232 | tf_op jit(solution)/shard_map/ppermute | solution.py:14
  1029.9 6.8 fusion.27
  (141 shorter events, 101.1 us)
Async XLA Ops:
  7.2 20.5 %copy-start = (bf16[1280,320]{0,1:T(8,128)(2,1)S(1)}, bf16[1280,320]{0,1:T(8,128)(2,1)}, u32[]{:S(2)}) copy-start(bf16[1280,320]{0,1:T(8,128)(2,1)} %param.15) | copy-start | bytes 2457604
  7.2 103.9 %all-reduce.4.cloned.1.call-start = ((), (), s32[]{:S(2)}) async-start(), calls=%async_computation | async-start | bytes 2097152 | tf_op jit(solution)/shard_map/psum | solution.py:82
  10.5 375.0 %all-gather.3.cloned.1.call-start = ((), (), s32[]{:S(2)}) async-start(), calls=%async_computation.1 | async-start | bytes 17825792 | tf_op jit(solution)/shard_map/all_gather | solution.py:68
  12.1 743.9 %all-reduce.6.cloned.1.call-start = ((), (), s32[]{:S(2)}) async-start(), calls=%async_computation.2 | async-start | bytes 4194304 | tf_op jit(solution)/shard_map/psum | solution.py:79
  12.1 130.4 %collective-permute-start.9 = (bf16[320,2048]{1,0:T(8,128)(2,1)S(1)}, bf16[320,2048]{1,0:T(8,128)(2,1)}, u32[]{:S(2)}, u32[]{:S(2)}) collective-permute-start(bf16[320,2048]{1,0:T(8,128)(2,1)S(1)} %copy-done.7), channel_id=1, source_target_pairs={{0,1},{1,0},{2,3},{3,2},{4,5},{5,4},{6,7},{7,6},{8,9},{9,8},{10,11... | collective-permute-start | bytes 3932168 | tf_op jit(solution)/shard_map/ppermute | solution.py:14
  12.7 142.9 %collective-permute-start.11 = (bf16[320,2048]{1,0:T(8,128)(2,1)S(1)}, bf16[320,2048]{1,0:T(8,128)(2,1)}, u32[]{:S(2)}, u32[]{:S(2)}) collective-permute-start(bf16[320,2048]{1,0:T(8,128)(2,1)S(1)} %copy-done.7), channel_id=1, source_target_pairs={{0,2},{2,0},{1,3},{3,1},{4,6},{6,4},{5,7},{7,5},{8,10},{10,8},{9,1... | collective-permute-start | bytes 3932168 | tf_op jit(solution)/shard_map/ppermute | solution.py:14
  15.3 102.7 %collective-permute-start = (bf16[320,2048]{1,0:T(8,128)(2,1)S(1)}, bf16[320,2048]{1,0:T(8,128)(2,1)}, u32[]{:S(2)}, u32[]{:S(2)}) collective-permute-start(bf16[320,2048]{1,0:T(8,128)(2,1)S(1)} %copy-done.6), channel_id=1, source_target_pairs={{0,1},{1,0},{2,3},{3,2},{4,5},{5,4},{6,7},{7,6},{8,9},{9,8},{10,11... | collective-permute-start | bytes 3932168 | tf_op jit(solution)/shard_map/ppermute | solution.py:14
  15.4 111.2 %collective-permute-start.1 = (bf16[320,2048]{1,0:T(8,128)(2,1)S(1)}, bf16[320,2048]{1,0:T(8,128)(2,1)}, u32[]{:S(2)}, u32[]{:S(2)}) collective-permute-start(bf16[320,2048]{1,0:T(8,128)(2,1)S(1)} %copy-done.6), channel_id=1, source_target_pairs={{0,2},{2,0},{1,3},{3,1},{4,6},{6,4},{5,7},{7,5},{8,10},{10,8},{9,1... | collective-permute-start | bytes 3932168 | tf_op jit(solution)/shard_map/ppermute | solution.py:14
  15.7 117.9 %collective-permute-start.2 = (bf16[320,2048]{1,0:T(8,128)(2,1)S(1)}, bf16[320,2048]{1,0:T(8,128)(2,1)}, u32[]{:S(2)}, u32[]{:S(2)}) collective-permute-start(bf16[320,2048]{1,0:T(8,128)(2,1)S(1)} %copy-done.6), channel_id=1, source_target_pairs={{0,4},{4,0},{1,5},{5,1},{2,6},{6,2},{3,7},{7,3},{8,12},{12,8},{9,1... | collective-permute-start | bytes 3932168 | tf_op jit(solution)/shard_map/ppermute | solution.py:14
  118.0 147.7 %collective-permute-start.13 = (bf16[320,2048]{1,0:T(8,128)(2,1)S(1)}, bf16[320,2048]{1,0:T(8,128)(2,1)S(1)}, u32[]{:S(2)}, u32[]{:S(2)}) collective-permute-start(bf16[320,2048]{1,0:T(8,128)(2,1)S(1)} %copy-done.7), channel_id=1, source_target_pairs={{0,4},{4,0},{1,5},{5,1},{2,6},{6,2},{3,7},{7,3},{8,12},{12,8},{9,1... | collective-permute-start | bytes 3932168 | tf_op jit(solution)/shard_map/ppermute | solution.py:14
  126.6 14.3 %collective-permute-start.8 = (bf16[320,1280]{1,0:T(8,128)(2,1)S(1)}, bf16[320,1280]{1,0:T(8,128)(2,1)S(1)}, u32[]{:S(2)}, u32[]{:S(2)}) collective-permute-start(bf16[320,1280]{1,0:T(8,128)(2,1)S(1)} %copy-done.24), channel_id=1, source_target_pairs={{0,1},{1,0},{2,3},{3,2},{4,5},{5,4},{6,7},{7,6},{8,9},{9,8},{10,11... | collective-permute-start | bytes 2457608 | tf_op jit(solution)/shard_map/ppermute | solution.py:14
  133.6 20.6 %collective-permute-start.10 = (bf16[320,1280]{1,0:T(8,128)(2,1)S(1)}, bf16[320,1280]{1,0:T(8,128)(2,1)S(1)}, u32[]{:S(2)}, u32[]{:S(2)}) collective-permute-start(bf16[320,1280]{1,0:T(8,128)(2,1)S(1)} %copy-done.23), channel_id=1, source_target_pairs={{0,2},{2,0},{1,3},{3,1},{4,6},{6,4},{5,7},{7,5},{8,10},{10,8},{9,1... | collective-permute-start | bytes 2457608 | tf_op jit(solution)/shard_map/ppermute | solution.py:14
  140.9 239.1 %collective-permute-start.15 = (bf16[320,2048]{1,0:T(8,128)(2,1)S(1)}, bf16[320,2048]{1,0:T(8,128)(2,1)S(1)}, u32[]{:S(2)}, u32[]{:S(2)}) collective-permute-start(bf16[320,2048]{1,0:T(8,128)(2,1)S(1)} %copy-done.7), channel_id=1, source_target_pairs={{0,8},{8,0},{1,9},{9,1},{2,10},{10,2},{3,11},{11,3},{4,12},{12,4},... | collective-permute-start | bytes 3932168 | tf_op jit(solution)/shard_map/ppermute | solution.py:14
  142.5 123.2 %collective-permute-start.12 = (bf16[320,1280]{1,0:T(8,128)(2,1)S(1)}, bf16[320,1280]{1,0:T(8,128)(2,1)S(1)}, u32[]{:S(2)}, u32[]{:S(2)}) collective-permute-start(bf16[320,1280]{1,0:T(8,128)(2,1)S(1)} %copy-done.22), channel_id=1, source_target_pairs={{0,4},{4,0},{1,5},{5,1},{2,6},{6,2},{3,7},{7,3},{8,12},{12,8},{9,1... | collective-permute-start | bytes 2457608 | tf_op jit(solution)/shard_map/ppermute | solution.py:14
  154.2 249.1 %collective-permute-start.3 = (bf16[320,2048]{1,0:T(8,128)(2,1)S(1)}, bf16[320,2048]{1,0:T(8,128)(2,1)}, u32[]{:S(2)}, u32[]{:S(2)}) collective-permute-start(bf16[320,2048]{1,0:T(8,128)(2,1)S(1)} %copy-done.6), channel_id=1, source_target_pairs={{0,8},{8,0},{1,9},{9,1},{2,10},{10,2},{3,11},{11,3},{4,12},{12,4},... | collective-permute-start | bytes 3932168 | tf_op jit(solution)/shard_map/ppermute | solution.py:14
  155.6 224.4 %collective-permute-start.14 = (bf16[320,1280]{1,0:T(8,128)(2,1)S(1)}, bf16[320,1280]{1,0:T(8,128)(2,1)S(1)}, u32[]{:S(2)}, u32[]{:S(2)}) collective-permute-start(bf16[320,1280]{1,0:T(8,128)(2,1)S(1)} %copy-done.21), channel_id=1, source_target_pairs={{0,8},{8,0},{1,9},{9,1},{2,10},{10,2},{3,11},{11,3},{4,12},{12,4},... | collective-permute-start | bytes 2457608 | tf_op jit(solution)/shard_map/ppermute | solution.py:14
  445.7 343.8 %collective-permute-start.4 = (bf16[1280,2048]{1,0:T(8,128)(2,1)}, bf16[1280,2048]{1,0:T(8,128)(2,1)}, u32[]{:S(2)}, u32[]{:S(2)}) collective-permute-start(bf16[1280,2048]{1,0:T(8,128)(2,1)} %get-tuple-element.13), channel_id=1, source_target_pairs={{0,1},{1,0},{2,3},{3,2},{4,5},{5,4},{6,7},{7,6},{8,9},{9,8},{10,11... | collective-permute-start | bytes 15728648 | tf_op jit(solution)/shard_map/ppermute | solution.py:14
  445.7 315.1 %collective-permute-start.5 = (bf16[1280,2048]{1,0:T(8,128)(2,1)}, bf16[1280,2048]{1,0:T(8,128)(2,1)}, u32[]{:S(2)}, u32[]{:S(2)}) collective-permute-start(bf16[1280,2048]{1,0:T(8,128)(2,1)} %get-tuple-element.13), channel_id=1, source_target_pairs={{0,2},{2,0},{1,3},{3,1},{4,6},{6,4},{5,7},{7,5},{8,10},{10,8},{9,1... | collective-permute-start | bytes 15728648 | tf_op jit(solution)/shard_map/ppermute | solution.py:14
  447.3 316.4 %collective-permute-start.6 = (bf16[1280,2048]{1,0:T(8,128)(2,1)}, bf16[1280,2048]{1,0:T(8,128)(2,1)}, u32[]{:S(2)}, u32[]{:S(2)}) collective-permute-start(bf16[1280,2048]{1,0:T(8,128)(2,1)} %get-tuple-element.13), channel_id=1, source_target_pairs={{0,4},{4,0},{1,5},{5,1},{2,6},{6,2},{3,7},{7,3},{8,12},{12,8},{9,1... | collective-permute-start | bytes 15728648 | tf_op jit(solution)/shard_map/ppermute | solution.py:14
  447.3 332.5 %collective-permute-start.7 = (bf16[1280,2048]{1,0:T(8,128)(2,1)}, bf16[1280,2048]{1,0:T(8,128)(2,1)}, u32[]{:S(2)}, u32[]{:S(2)}) collective-permute-start(bf16[1280,2048]{1,0:T(8,128)(2,1)} %get-tuple-element.13), channel_id=1, source_target_pairs={{0,8},{8,0},{1,9},{9,1},{2,10},{10,2},{3,11},{11,3},{4,12},{12,4},... | collective-permute-start | bytes 15728648 | tf_op jit(solution)/shard_map/ppermute | solution.py:14
  464.7 346.6 %collective-permute-start.19 = (bf16[1280,2048]{1,0:T(8,128)(2,1)}, bf16[1280,2048]{1,0:T(8,128)(2,1)}, u32[]{:S(2)}, u32[]{:S(2)}) collective-permute-start(bf16[1280,2048]{1,0:T(8,128)(2,1)} %get-tuple-element.12), channel_id=1, source_target_pairs={{0,2},{2,0},{1,3},{3,1},{4,6},{6,4},{5,7},{7,5},{8,10},{10,8},{9,1... | collective-permute-start | bytes 15728648 | tf_op jit(solution)/shard_map/ppermute | solution.py:14
  507.4 251.2 %copy-start.25 = (bf16[320,128]{1,0:T(8,128)(2,1)S(1)}, bf16[320,128]{1,0:T(8,128)(2,1)}, u32[]{:S(2)}) copy-start(bf16[320,128]{1,0:T(8,128)(2,1)} %param.21) | copy-start | bytes 245764
  760.9 260.1 %collective-permute-start.21 = (bf16[1280,2048]{1,0:T(8,128)(2,1)}, bf16[1280,2048]{1,0:T(8,128)(2,1)S(1)}, u32[]{:S(2)}, u32[]{:S(2)}) collective-permute-start(bf16[1280,2048]{1,0:T(8,128)(2,1)} %get-tuple-element.12), channel_id=1, source_target_pairs={{0,4},{4,0},{1,5},{5,1},{2,6},{6,2},{3,7},{7,3},{8,12},{12,8},{9,1... | collective-permute-start | bytes 15728648 | tf_op jit(solution)/shard_map/ppermute | solution.py:14
  763.7 261.7 %collective-permute-start.23 = (bf16[1280,2048]{1,0:T(8,128)(2,1)}, bf16[1280,2048]{1,0:T(8,128)(2,1)}, u32[]{:S(2)}, u32[]{:S(2)}) collective-permute-start(bf16[1280,2048]{1,0:T(8,128)(2,1)} %get-tuple-element.12), channel_id=1, source_target_pairs={{0,8},{8,0},{1,9},{9,1},{2,10},{10,2},{3,11},{11,3},{4,12},{12,4},... | collective-permute-start | bytes 15728648 | tf_op jit(solution)/shard_map/ppermute | solution.py:14
  779.8 256.9 %collective-permute-start.17 = (bf16[1280,2048]{1,0:T(8,128)(2,1)}, bf16[1280,2048]{1,0:T(8,128)(2,1)S(1)}, u32[]{:S(2)}, u32[]{:S(2)}) collective-permute-start(bf16[1280,2048]{1,0:T(8,128)(2,1)} %get-tuple-element.12), channel_id=1, source_target_pairs={{0,1},{1,0},{2,3},{3,2},{4,5},{5,4},{6,7},{7,6},{8,9},{9,8},{10,11... | collective-permute-start | bytes 15728648 | tf_op jit(solution)/shard_map/ppermute | solution.py:14
  789.5 20.7 %collective-permute-start.18 = (bf16[1280,320]{0,1:T(8,128)(2,1)S(1)}, bf16[1280,320]{0,1:T(8,128)(2,1)S(1)}, u32[]{:S(2)}, u32[]{:S(2)}) collective-permute-start(bf16[1280,320]{0,1:T(8,128)(2,1)S(1)} %copy-done.20), channel_id=1, source_target_pairs={{0,2},{2,0},{1,3},{3,1},{4,6},{6,4},{5,7},{7,5},{8,10},{10,8},{9,1... | collective-permute-start | bytes 2457608 | tf_op jit(solution)/shard_map/ppermute | solution.py:14
  796.3 13.8 %copy-start.19 = (bf16[1280,320]{0,1:T(8,128)(2,1)S(1)}, bf16[1280,320]{0,1:T(8,128)(2,1)}, u32[]{:S(2)}) copy-start(bf16[1280,320]{0,1:T(8,128)(2,1)} %get-tuple-element.16) | copy-start | bytes 2457604
  796.4 14.9 %copy-start.18 = (bf16[1280,320]{0,1:T(8,128)(2,1)S(1)}, bf16[1280,320]{0,1:T(8,128)(2,1)}, u32[]{:S(2)}) copy-start(bf16[1280,320]{0,1:T(8,128)(2,1)} %get-tuple-element.15) | copy-start | bytes 2457604
  810.2 210.8 %collective-permute-start.20 = (bf16[1280,320]{0,1:T(8,128)(2,1)S(1)}, bf16[1280,320]{0,1:T(8,128)(2,1)S(1)}, u32[]{:S(2)}, u32[]{:S(2)}) collective-permute-start(bf16[1280,320]{0,1:T(8,128)(2,1)S(1)} %copy-done.19), channel_id=1, source_target_pairs={{0,4},{4,0},{1,5},{5,1},{2,6},{6,2},{3,7},{7,3},{8,12},{12,8},{9,1... | collective-permute-start | bytes 2457608 | tf_op jit(solution)/shard_map/ppermute | solution.py:14
  811.3 214.2 %collective-permute-start.22 = (bf16[1280,320]{0,1:T(8,128)(2,1)S(1)}, bf16[1280,320]{0,1:T(8,128)(2,1)S(1)}, u32[]{:S(2)}, u32[]{:S(2)}) collective-permute-start(bf16[1280,320]{0,1:T(8,128)(2,1)S(1)} %copy-done.18), channel_id=1, source_target_pairs={{0,8},{8,0},{1,9},{9,1},{2,10},{10,2},{3,11},{11,3},{4,12},{12,4},... | collective-permute-start | bytes 2457608 | tf_op jit(solution)/shard_map/ppermute | solution.py:14
  816.5 204.5 %copy-start.17 = (bf16[1280,320]{0,1:T(8,128)(2,1)S(1)}, bf16[1280,320]{0,1:T(8,128)(2,1)}, u32[]{:S(2)}) copy-start(bf16[1280,320]{0,1:T(8,128)(2,1)} %get-tuple-element.14) | copy-start | bytes 2457604
  1021.0 15.7 %collective-permute-start.16 = (bf16[1280,320]{0,1:T(8,128)(2,1)S(1)}, bf16[1280,320]{0,1:T(8,128)(2,1)S(1)}, u32[]{:S(2)}, u32[]{:S(2)}) collective-permute-start(bf16[1280,320]{0,1:T(8,128)(2,1)S(1)} %copy-done.17), channel_id=1, source_target_pairs={{0,1},{1,0},{2,3},{3,2},{4,5},{5,4},{6,7},{7,6},{8,9},{9,8},{10,11... | collective-permute-start | bytes 2457608 | tf_op jit(solution)/shard_map/ppermute | solution.py:14
  (26 other events, 155.6 us)
Sparse Core Ops, SparseCore 0:
  12.1 98.9 all-reduce.3
  113.8 245.6 all-gather.2
  465.1 290.8 all-reduce.5
